TPU v7x, 128 devices: a whole 4x4x4 slice. The times are simulated.
128 devices in a mesh: dp: 16 (over y, z_hi, core), space: 8 (over x, z_lo).
Axes of the slice: x: 4, y: 4, z: 4 (z_hi: 2, z_lo: 2; z = z_hi * 2 + z_lo), core: 2. Of those that a mesh axis runs over, the one named last changes fastest.
Arguments:
- inputs: bfloat16 [128, 32, 32, 1024], P('dp', None, 'space'), may hold values from 0 to 2
- conv_in: bfloat16 [64, 864], replicated, may hold values from -0.21875 to 0.21875
- norm_gain: float32 [64], replicated, may hold values from 0.5 to 1.5
- norm_shift: float32 [64], replicated, may hold values from -3 to 3
- conv_out: bfloat16 [128, 1728], replicated, may hold values from -0.15625 to 0.15625
- dense_in: bfloat16 [65536, 128], replicated, may hold values from -0.0234375 to 0.0234375
- dense_out: bfloat16 [128, 4], replicated, may hold values from -0.5 to 0.5
- targets: float32 [128, 4], P(('dp', 'space')), may hold values from -6 to 6
Outputs:
- grad_conv_in: float32 [64, 864], replicated
- grad_norm: float32 [2, 64], replicated
- grad_conv_out: float32 [128, 1728], replicated
- grad_dense_in: float32 [65536, 128], P(('dp', 'space'))
- grad_dense_out: float32 [128, 4], replicated
- predictions: float32 [128, 4], P(('dp', 'space'))
All inputs are finite; a program needn't handle non-finite values.
Results may differ from a plain program's by a relative error of at most 0.015.
Values may be sent and summed in bfloat16 or wider, within the bound.
A program may use at most 256 MiB of HBM per device.

v0:
```python
import jax
import jax.numpy as jnp
from jax import lax
from jax.sharding import PartitionSpec as P

C_OUT = 128
GRID = 32
norm_epsilon = 1e-05


def extended_2(cells, sides, width):
    for axis, dim in sides:
        count = lax.axis_size(axis)
        ends = count - 1
        head = lax.slice_in_dim(cells, 0, width, axis=dim)
        tail = lax.slice_in_dim(cells, cells.shape[dim] - width, cells.shape[dim], axis=dim)
        cells = jnp.concatenate(
            [
                lax.ppermute(tail, axis, [(i, (i + 1) % count) for i in range(ends)]),
                cells,
                lax.ppermute(head, axis, [((i + 1) % count, i) for i in range(ends)]),
            ],
            axis=dim,
        )
    return cells


def leaky_relu(values):
    return 0.65 * values + 0.35 * values * jnp.tanh(values)


def slope_of(values):
    bent = jnp.tanh(values)
    return 0.65 + 0.35 * (bent + values * (1.0 - bent * bent))


def plane_shift(volume, step_y, step_z, extent):
    plane_len = extent * extent
    offset = step_y * extent + step_z
    margin = extent + 1
    pad_widths = [(0, 0)] * (volume.ndim - 1) + [(margin, margin)]
    padded = jnp.pad(volume, pad_widths)
    shifted = lax.slice_in_dim(
        padded, margin + offset, margin + offset + plane_len, axis=volume.ndim - 1
    )
    column = lax.broadcasted_iota(jnp.int32, (plane_len,), 0) % extent
    inside = ((column + step_z >= 0) & (column + step_z < extent)).astype(volume.dtype)
    return shifted * inside


def columns(slab_ext, planes, extent):
    pieces = []
    for step_x in (-1, 0, 1):
        plane_set = lax.slice_in_dim(slab_ext, 1 + step_x, 1 + step_x + planes, axis=1)
        for step_y in (-1, 0, 1):
            for step_z in (-1, 0, 1):
                pieces.append(plane_shift(plane_set, step_y, step_z, extent))
    stacked = jnp.stack(pieces, 0)
    return stacked.reshape(len(pieces) * slab_ext.shape[0], planes * extent * extent)


def pad_planes(volume, extent):
    shaped = volume.reshape(volume.shape[0], extent, extent * extent)
    return jnp.pad(shaped, ((0, 0), (1, 1), (0, 0)))


def pool_slab(active, planes, extent):
    samples, channels = (active.shape[0], active.shape[1])
    blocks = active.reshape(samples, channels, planes // 2, 2, extent // 2, 2, extent // 2, 2)
    return (blocks.sum(axis=(3, 5, 7)) * 0.125).reshape(samples, channels, -1)


def unpool_slab(gradient, planes, extent):
    samples, channels = (gradient.shape[0], gradient.shape[1])
    blocks = gradient.reshape(samples, channels, planes // 2, 1, extent // 2, 1, extent // 2, 1)
    wide = jnp.broadcast_to(
        blocks, (samples, channels, planes // 2, 2, extent // 2, 2, extent // 2, 2)
    )
    return wide.reshape(samples, channels, planes * extent * extent) * 0.125


def shards(inputs, conv_in, norm_gain, norm_shift, conv_out, dense_in, dense_out, targets):
    half_grid = GRID // 2
    quarter = GRID // 4
    cell_count = inputs.shape[0] * GRID**3
    extended = extended_2(inputs, (("space", 2),), 1)
    planes = extended.shape[2] - 2

    def first_conv(slab_ext):
        return jnp.dot(conv_in, columns(slab_ext, planes, GRID), preferred_element_type=jnp.float32)

    first_out = lax.map(first_conv, extended)
    local_sum = jnp.sum(first_out, axis=(0, 2))
    average = lax.psum(local_sum, "space") / cell_count
    centred = first_out - average[None, :, None]
    variance = lax.psum(jnp.sum(centred * centred, axis=(0, 2)), "space") / cell_count
    inverse = lax.rsqrt(variance + norm_epsilon)
    whitened = centred * inverse[None, :, None]
    normed = norm_gain[None, :, None] * whitened + norm_shift[None, :, None]
    pooled = pool_slab(leaky_relu(normed), planes, GRID).astype(jnp.bfloat16)
    samples_pooled = lax.all_to_all(pooled, "space", split_axis=0, concat_axis=2, tiled=True)

    def second_conv(volume):
        return jnp.dot(
            conv_out,
            columns(pad_planes(volume, half_grid), half_grid, half_grid),
            preferred_element_type=jnp.float32,
        )

    second_out = lax.map(second_conv, samples_pooled)
    local_samples = second_out.shape[0]
    features = (
        pool_slab(leaky_relu(second_out), half_grid, half_grid)
        .reshape(local_samples, -1)
        .astype(jnp.bfloat16)
    )
    hidden_pre = jnp.dot(features, dense_in, preferred_element_type=jnp.float32)
    hidden = leaky_relu(hidden_pre).astype(jnp.bfloat16)
    predictions = jnp.dot(hidden, dense_out, preferred_element_type=jnp.float32)
    misfit = predictions - targets
    grad_out_local = jnp.dot(hidden.astype(jnp.float32).T, misfit, precision=lax.Precision.HIGHEST)
    back_hidden = (
        jnp.dot(misfit, dense_out.astype(jnp.float32).T, precision=lax.Precision.HIGHEST)
        * slope_of(hidden_pre)
    ).astype(jnp.bfloat16)
    grad_dense_in = lax.psum_scatter(
        lax.dot_general(
            features, back_hidden, (((0,), (0,)), ((), ())), preferred_element_type=jnp.float32
        ),
        ("dp", "space"),
        scatter_dimension=0,
        tiled=True,
    )
    back_features = lax.dot_general(
        back_hidden, dense_in, (((1,), (1,)), ((), ())), preferred_element_type=jnp.float32
    )
    back_features = back_features.reshape(local_samples, C_OUT, quarter**3)
    back_second = (unpool_slab(back_features, half_grid, half_grid) * slope_of(second_out)).astype(
        jnp.bfloat16
    )

    def second_back(running, couple):
        volume, gradient = couple
        padded = pad_planes(volume, half_grid)
        patches = columns(padded, half_grid, half_grid)
        running = running + lax.dot_general(
            gradient, patches, (((1,), (1,)), ((), ())), preferred_element_type=jnp.float32
        )
        patch_grad = lax.dot_general(
            conv_out, gradient, (((0,), (0,)), ((), ())), preferred_element_type=jnp.float32
        )
        _, unfold = jax.vjp(
            lambda whole_pad: columns(whole_pad, half_grid, half_grid), padded.astype(jnp.float32)
        )
        volume_grad = unfold(patch_grad)[0][:, 1:-1, :]
        return (running, volume_grad.reshape(volume.shape).astype(jnp.bfloat16))

    grad_conv_out, back_pooled = lax.scan(
        second_back, jnp.zeros(conv_out.shape, jnp.float32), (samples_pooled, back_second)
    )
    back_slab = lax.all_to_all(back_pooled, "space", split_axis=2, concat_axis=0, tiled=True)
    back_active = unpool_slab(back_slab.astype(jnp.float32), planes, GRID) * slope_of(normed)
    sum_grad = jnp.sum(back_active, axis=(0, 2))
    sum_xgrad = jnp.sum(back_active * whitened, axis=(0, 2))
    group_grad, group_xgrad = lax.psum((sum_grad, sum_xgrad), "space")
    back_first = (norm_gain * inverse)[None, :, None] * (
        back_active
        - group_grad[None, :, None] / cell_count
        - whitened * group_xgrad[None, :, None] / cell_count
    )
    back_first = back_first.astype(jnp.bfloat16)

    def first_back(running, couple):
        slab_ext, gradient = couple
        patches = columns(slab_ext, planes, GRID)
        return (
            running
            + lax.dot_general(
                gradient, patches, (((1,), (1,)), ((), ())), preferred_element_type=jnp.float32
            ),
            None,
        )

    grad_conv_in, _ = lax.scan(
        first_back, jnp.zeros(conv_in.shape, jnp.float32), (extended, back_first)
    )
    grad_norm_local = jnp.stack([sum_xgrad, sum_grad])
    summed = lax.psum(
        (grad_conv_in, grad_norm_local, grad_conv_out, grad_out_local), ("dp", "space")
    )
    return (summed[0], summed[1], summed[2], grad_dense_in, summed[3], predictions)


def solution(mesh):
    placed = (P("dp", None, "space", None), P(), P(), P(), P(), P(), P(), P(("dp", "space"), None))
    return jax.shard_map(
        shards,
        mesh=mesh,
        in_specs=placed,
        out_specs=(P(), P(), P(), P(("dp", "space"), None), P(), P(("dp", "space"), None)),
        check_vma=False,
    )
```

profile of v0, /device:TPU:0, one launch (start us, length us, event | category | flops | bytes accessed | tf_op | source)
XLA Modules:
  0.0 1617.1 jit_solution(11225034496510748048)
XLA Ops:
  19.1 8.3 collective-permute-done.1
  29.4 9.5 collective-permute-done
  45.6 131.2 %while.34 = (s32[]{:T(128)}, f32[8,64,4096]{2,1,0:T(8,128)}, bf16[8,32,6,1024]{3,2,1,0:T(8,128)(2,1)}, bf16[64,864]{1,0:T(8,128)(2,1)}, s32[]{:T(128)}) while((s32[]{:T(128)}, f32[8,64,4096]{2,1,0:T(8,128)}, bf16[8,32,6,1024]{3,2,1,0:T(8,128)(2,1)}, bf16[64,864]{1,0:T(8,128)(2,1)}, s32[]{:T(128)}) %tuple.124), condition=%wide.region_1.2_spmd, body=%wide.region_0.1_spmd.sunk | while | flops 467173376 | bytes 38973516 | solution.py:92
  176.8 12.3 copy.39
  193.1 19.2 %psum.56 = f32[64]{0:T(128)S(1)} all-reduce(f32[64]{0:T(128)S(1)} %reduce_sum.54), channel_id=1, replica_groups=mesh['dp'=16,'space'=8] {'space'}, use_global_device_ids=true, to_apply=%region_3.4 | all-reduce | flops 64 | bytes 512 | tf_op jit(solution)/shard_map/psum | solution.py:94
  212.3 8.1 multiply_reduce_fusion.1
  220.4 16.4 %psum.57 = f32[64]{0:T(128)S(1)} all-reduce(f32[64]{0:T(128)S(1)} %multiply_reduce_fusion.1), channel_id=1, replica_groups=mesh['dp'=16,'space'=8] {'space'}, use_global_device_ids=true, to_apply=%region_5.6 | all-reduce | flops 64 | bytes 512 | tf_op jit(solution)/shard_map/psum | solution.py:96
  236.8 12.9 fusion.38
  306.3 78.6 %fusion.140 = f32[1,128,8,8,8]{4,0,3,2,1:T(1,128)} fusion(bf16[128,8,8,8,128]{4,3,2,1,0:T(8,128)(2,1)} %bitcast.529, bf16[128]{0:T(256)(128)(2,1)S(1)} %get-tuple-element.270), kind=kOutput, calls=%fused_computation.309 | convolution fusion | flops 16777216 | bytes 17039616 | tf_op jit(solution)/shard_map/dot_general | solution.py:134
  384.9 8.7 copy.49
  397.7 11.3 convolution_bitcast_fusion.1
  415.2 11.4 fusion.156
  473.5 8.7 fusion.58
  489.5 24.4 %reduce.1 = bf16[4096,64]{1,0:T(8,128)(2,1)} reduce(bf16[4096,1,64]{2,1,0:T(2,128)(2,1)} %bitcast.534, bf16[]{:T(256)} %broadcast.801), dimensions={1}, to_apply=%bitcast.376.reduce_sub_computation | reduce | bytes 1048578
  520.6 10.0 fusion.160
  538.2 11.5 fusion.39
  549.7 20.0 %all-reduce.39 = (f32[64]{0:T(128)S(1)}, f32[64]{0:T(128)S(1)}) all-reduce(f32[64]{0:T(128)S(1)} %get-tuple-element.176, f32[64]{0:T(128)S(1)} %get-tuple-element.175), channel_id=1, replica_groups=mesh['dp'=16,'space'=8] {'space'}, use_global_device_ids=true, to_apply=%region_11.12 | all-reduce | flops 128 | bytes 1024 | tf_op jit(solution)/shard_map/psum | solution.py:165
  569.6 14.0 multiply_convert_fusion
  583.7 9.8 copy.47
  593.4 136.7 %while.35 = (s32[]{:T(128)}, f32[64,864]{1,0:T(8,128)}, bf16[8,64,4096]{2,1,0:T(8,128)(2,1)}, bf16[8,32,6,1024]{3,2,1,0:T(8,128)(2,1)}, s32[]{:T(128)}, /*index=5*/s32[]{:T(128)}) while((s32[]{:T(128)}, f32[64,864]{1,0:T(8,128)}, bf16[8,64,4096]{2,1,0:T(8,128)(2,1)}, bf16[8,32,6,1024]{3,2,1,0:T(8,128)(2,1)}, s32[]{:T(128)}, ...), condition=%wide.region_13.14_spmd.clone, body=%wide.region_12.13_spmd.clone.sunk | while | flops 467283968 | bytes 40546452 | solution.py:184
  730.2 25.5 %broadcast_multiply_fusion = f32[65536,128]{1,0:T(8,128)} fusion(f32[128]{0:T(128)S(1)} %copy-done.25, f32[65536]{0:T(1024)} %convert.13), kind=kLoop, calls=%fused_computation.102 | loop fusion | flops 8388608 | bytes 33817088 | tf_op jit(solution)/shard_map/dot_general | solution.py:127
  756.5 64.4 %all-reduce.37 = (f32[2,64]{1,0:T(2,128)}, f32[128,4]{0,1:T(4,128)}) all-reduce(f32[2,64]{1,0:T(2,128)S(1)} %pad_maximum_fusion.1, f32[128,4]{0,1:T(4,128)S(1)} %broadcast_multiply_fusion.1), channel_id=1, replica_groups=mesh['dp'=16,'space'=8] {'dp','space'}, use_global_device_ids=true, to_apply=%region_15.16 | all-reduce | flops 640 | bytes 5120 | tf_op jit(solution)/shard_map/psum | solution.py:188
  820.8 56.8 %all-reduce.42.cloned.1.call-done = (f32[64,864]{1,0:T(8,128)}, f32[128,1728]{0,1:T(8,128)}) async-done(((f32[64,864]{1,0:T(8,128)}, f32[128,1728]{0,1:T(8,128)}), (f32[64,864]{1,0:T(8,128)}, f32[128,1728]{0,1:T(8,128)})) %all-reduce.42.cloned.1.call-update) | async-done | bytes 1105936 | tf_op jit(solution)/shard_map/psum | solution.py:188
  877.7 728.4 %reduce-scatter.2.cloned.1.call-done = f32[512,128]{1,0:T(8,128)} async-done(((f32[65536,128]{1,0:T(8,128)}), f32[512,128]{1,0:T(8,128)}) %reduce-scatter.2.cloned.1.call-update) | async-done | bytes 262160 | tf_op jit(solution)/shard_map/reduce_scatter | solution.py:126
  (755 shorter events, 429.3 us)
Async XLA Ops:
  7.2 278.6 %copy-start = (bf16[128,1728]{0,1:T(8,128)(2,1)S(1)}, bf16[128,1728]{0,1:T(8,128)(2,1)}, u32[]{:S(2)}) copy-start(bf16[128,1728]{0,1:T(8,128)(2,1)} %param.16) | copy-start | bytes 1327108
  7.2 33.6 %copy-start.3 = (bf16[8,32,4,1024]{3,2,1,0:T(4,128)(2,1)S(1)}, bf16[8,32,4,1024]{3,2,1,0:T(4,128)(2,1)}, u32[]{:S(2)}) copy-start(bf16[8,32,4,1024]{3,2,1,0:T(4,128)(2,1)} %param.12) | copy-start | bytes 6291460
  11.5 15.9 collective-permute-start.1
  13.8 25.1 %collective-permute-start = (bf16[8,32,1,1024]{3,1,2,0:T(8,128)(2,1)}, bf16[8,32,1,1024]{3,1,2,0:T(8,128)(2,1)}, u32[]{:S(2)}, u32[]{:S(2)}) collective-permute-start(bf16[8,32,1,1024]{3,1,2,0:T(8,128)(2,1)} %copy.52), channel_id=1, source_target_pairs={{0,1},{1,2},{2,3},{3,4},{4,5},{5,6},{6,7},{8,9},{9,10},{10,11},{11... | collective-permute-start | bytes 1572872 | tf_op jit(solution)/shard_map/ppermute | solution.py:19
  212.3 24.5 %copy-start.22 = (f32[64]{0:T(128)S(1)}, f32[64]{0:T(128)}, u32[]{:S(2)}) copy-start(f32[64]{0:T(128)} %param.14) | copy-start | bytes 772
  212.3 24.5 %copy-start.23 = (f32[64]{0:T(128)S(1)}, f32[64]{0:T(128)}, u32[]{:S(2)}) copy-start(f32[64]{0:T(128)} %param.15) | copy-start | bytes 772
  261.4 11.6 all-to-all-start
  285.7 5.7 copy-start.2
  298.0 7.5 copy-start.26
  298.0 7.6 copy-start.27
  305.6 79.2 %copy-start.29 = (f32[1,4]{1,0:T(1,128)}, f32[1,4]{1,0:T(1,128)S(1)}, u32[]{:S(2)}) copy-start(f32[1,4]{1,0:T(1,128)S(1)} %fusion.150) | copy-start | bytes 52
  426.6 6.0 copy-start.19
  427.9 6.0 copy-start.17
  432.6 6.3 copy-start.13
  434.6 7.2 copy-start.11
  435.9 6.2 copy-start.10
  436.3 7.2 copy-start.9
  437.6 7.2 copy-start.8
  438.8 7.2 copy-start.7
  517.1 16.4 %all-to-all-start.1 = ((bf16[8,2,16384]{2,1,0:T(2,128)(2,1)}), bf16[8,2,16384]{2,1,0:T(2,128)(2,1)S(1)}, u32[]{:S(2)}, u32[]{:S(2)}) async-start(bf16[8,2,16384]{2,1,0:T(2,128)(2,1)} %reshape.342), calls=%async_computation.1 | async-start | bytes 1048576 | tf_op jit(solution)/shard_map/all_to_all | solution.py:161
  520.6 357.1 %all-reduce.42.cloned.1.call-start = ((), (), s32[]{:S(2)}) async-start(), calls=%async_computation.4 | async-start | bytes 2228224 | tf_op jit(solution)/shard_map/psum | solution.py:188
  593.4 136.7 %copy-start.25 = (f32[128]{0:T(128)S(1)}, f32[128]{0:T(128)}, u32[]{:S(2)}) copy-start(f32[128]{0:T(128)} %get-tuple-element.269) | copy-start | bytes 1540
  730.1 875.9 %reduce-scatter.2.cloned.1.call-start = ((), (), s32[]{:S(2)}) async-start(), calls=%async_computation.3 | async-start | bytes 33816576 | tf_op jit(solution)/shard_map/reduce_scatter | solution.py:126
  756.4 853.4 %copy-start.1 = (bf16[128,1728]{0,1:T(8,128)(2,1)S(1)}, bf16[128,1728]{0,1:T(8,128)(2,1)}, u32[]{:S(2)}) copy-start(bf16[128,1728]{0,1:T(8,128)(2,1)} %param.16) | copy-start | bytes 1327108
  (27 other events, 78.8 us)
Sparse Core Ops, SparseCore 0:
  730.2 147.3 all-reduce.41
  880.8 725.2 reduce-scatter.1
where the time goes:
time: 1620 us
  waiting for transfers between devices  811 us (50%)
  other arithmetic  267 us (16%)
  local copies, waits for them, and re-layouts  221 us (14%)
  matrix products  167 us (10%)
  blocking collectives  120 us (7%)
    reduce_scatter x1, waiting for transfers between devices, shards(): lax.psum_scatter(lax.dot_general(features, back_hidden, (((0,), (0,)), ((...  728 us
    while x416, other arithmetic  107 us
    while x48, local copies, waits for them, and re-layouts  79.7 us
    dot_general x1, matrix products, shards(): lax.dot_general(back_hidden, dense_in, (((1,), (1,)), ((), ())), preferre...  78.6 us
    psum x1, blocking collectives, shards(): lax.psum((grad_conv_in, grad_norm_local, grad_conv_out, grad_out_local),...  64.4 us
    psum x1, waiting for transfers between devices, shards(): lax.psum((grad_conv_in, grad_norm_local, grad_conv_out, grad_out_local),...  56.8 us
    unnamed x94, local copies, waits for them, and re-layouts  53.9 us
  transfers between devices with their start and end apart: 6, of which 5 were waited for; matrix products, arithmetic and copies ran while one was open for 3% of the time, Pallas kernels for 0%

commit v1 on v0

--- a/solution.py
+++ b/solution.py
@@ -186,7 +186,7 @@
     )
     grad_norm_local = jnp.stack([sum_xgrad, sum_grad])
     summed = lax.psum(
-        (grad_conv_in, grad_norm_local, grad_conv_out, grad_out_local), ("dp", "space")
+        lax.psum((grad_conv_in, grad_norm_local, grad_conv_out, grad_out_local), "space"), "dp"
     )
     return (summed[0], summed[1], summed[2], grad_dense_in, summed[3], predictions)
 

time: 1620 us -> 1590 us (0.981)
  blocking collectives: 120 us -> 90.2 us
    reduce_scatter x1, waiting for transfers between devices: 728 us -> 558 us  [shards(): lax.psum_scatter(lax.dot_general(features, back_hidden, (((0,), (0,)), ((...]
    psum x0 -> x1, waiting for transfers between devices: none -> 148 us  [shards(): lax.psum(lax.psum((grad_conv_in, grad_norm_local, grad_conv_out, grad_out...]
    psum x1, blocking collectives: 64.4 us -> 34.6 us  [shards(): lax.psum(lax.psum((grad_conv_in, grad_norm_local, grad_conv_out, grad_out...]
    psum x1, waiting for transfers between devices: 56.8 us -> 74.8 us  [shards(): lax.psum((grad_conv_in, grad_norm_local, grad_conv_out, grad_out_local),...]
  transfers between devices with their start and end apart: 6 -> 7, of which waited for: 5 -> 6; matrix products, arithmetic and copies ran while one was open for 3% -> 3% of each run, Pallas kernels for 0% -> 0%
where the time goes in v1:
time: 1590 us; the launch traced here: 1570 us
  waiting for transfers between devices  807 us (51%)
  other arithmetic  264 us (17%)
  local copies, waits for them, and re-layouts  215 us (14%)
  matrix products  166 us (10%)
  blocking collectives  90.2 us (6%)
  between operations  16.6 us (1%)
    reduce_scatter x1, waiting for transfers between devices, shards(): lax.psum_scatter(lax.dot_general(features, back_hidden, (((0,), (0,)), ((...  558 us
    psum x1, waiting for transfers between devices, shards(): lax.psum(lax.psum((grad_conv_in, grad_norm_local, grad_conv_out, grad_out...  148 us
    while x416, other arithmetic  107 us
    while x48, local copies, waits for them, and re-layouts  79.7 us
    dot_general x1, matrix products, shards(): lax.dot_general(back_hidden, dense_in, (((1,), (1,)), ((), ())), preferre...  78.3 us
    psum x1, waiting for transfers between devices, shards(): lax.psum((grad_conv_in, grad_norm_local, grad_conv_out, grad_out_local),...  74.8 us
    unnamed x94, local copies, waits for them, and re-layouts  49.2 us
    psum x1, blocking collectives, shards(): lax.psum(lax.psum((grad_conv_in, grad_norm_local, grad_conv_out, grad_out...  34.6 us
  transfers between devices with their start and end apart: 7, of which 6 were waited for; matrix products, arithmetic and copies ran while one was open for 3% of the time, Pallas kernels for 0%

profile of v1, /device:TPU:0, one launch (start us, length us, event | category | flops | bytes accessed | tf_op | source)
XLA Modules:
  0.0 1574.8 jit_solution(11948206350887267564)
XLA Ops:
  19.9 8.3 collective-permute-done.1
  30.2 9.5 collective-permute-done
  46.4 131.2 %while.34 = (s32[]{:T(128)}, f32[8,64,4096]{2,1,0:T(8,128)}, bf16[8,32,6,1024]{3,2,1,0:T(8,128)(2,1)}, bf16[64,864]{1,0:T(8,128)(2,1)}, s32[]{:T(128)}) while((s32[]{:T(128)}, f32[8,64,4096]{2,1,0:T(8,128)}, bf16[8,32,6,1024]{3,2,1,0:T(8,128)(2,1)}, bf16[64,864]{1,0:T(8,128)(2,1)}, s32[]{:T(128)}) %tuple.124), condition=%wide.region_1.2_spmd, body=%wide.region_0.1_spmd.sunk | while | flops 467173376 | bytes 38973516 | solution.py:92
  177.6 12.3 copy.39
  193.9 19.2 %psum.84 = f32[64]{0:T(128)S(1)} all-reduce(f32[64]{0:T(128)S(1)} %reduce_sum.54), channel_id=1, replica_groups=mesh['dp'=16,'space'=8] {'space'}, use_global_device_ids=true, to_apply=%region_3.4 | all-reduce | flops 64 | bytes 512 | tf_op jit(solution)/shard_map/psum | solution.py:94
  221.2 16.4 %psum.85 = f32[64]{0:T(128)S(1)} all-reduce(f32[64]{0:T(128)S(1)} %multiply_reduce_fusion.1), channel_id=1, replica_groups=mesh['dp'=16,'space'=8] {'space'}, use_global_device_ids=true, to_apply=%region_5.6 | all-reduce | flops 64 | bytes 512 | tf_op jit(solution)/shard_map/psum | solution.py:96
  237.7 12.9 fusion.38
  306.9 78.3 %fusion.140 = f32[1,128,8,8,8]{4,0,3,2,1:T(1,128)} fusion(bf16[128,8,8,8,128]{4,3,2,1,0:T(8,128)(2,1)} %bitcast.529, bf16[128]{0:T(256)(128)(2,1)S(1)} %get-tuple-element.274), kind=kOutput, calls=%fused_computation.309 | convolution fusion | flops 16777216 | bytes 17039616 | tf_op jit(solution)/shard_map/dot_general | solution.py:134
  385.3 8.9 copy.49
  396.6 11.2 convolution_bitcast_fusion.1
  413.7 11.7 fusion.156
  465.6 8.7 fusion.58
  478.3 23.4 %reduce.1 = bf16[4096,64]{1,0:T(8,128)(2,1)} reduce(bf16[4096,1,64]{2,1,0:T(2,128)(2,1)S(1)} %bitcast.534, bf16[]{:T(256)} %broadcast.801), dimensions={1}, to_apply=%bitcast.376.reduce_sub_computation | reduce | bytes 1048578
  508.6 10.0 fusion.160
  523.4 11.5 fusion.39
  534.9 20.0 %all-reduce.39 = (f32[64]{0:T(128)S(1)}, f32[64]{0:T(128)S(1)}, f32[2,64]{1,0:T(2,128)S(1)}, f32[128,4]{0,1:T(4,128)S(1)}) all-reduce(f32[64]{0:T(128)S(1)} %get-tuple-element.176, f32[64]{0:T(128)S(1)} %get-tuple-element.175, f32[2,64]{1,0:T(2,128)S(1)} %pad_maximum_fusion.1, ...), channel_id=1, replica_groups=mesh['dp'=16,'space'=8] {'space'}, use_global_device_ids=true, to_apply=%region_11.12 | all-reduce | flops 768 | bytes 6144 | tf_op jit(solution)/shard_map/psum | solution.py:165
  554.9 14.0 multiply_convert_fusion
  568.9 9.8 copy.47
  578.7 136.6 %while.35 = (s32[]{:T(128)}, f32[64,864]{1,0:T(8,128)}, bf16[8,64,4096]{2,1,0:T(8,128)(2,1)}, bf16[8,32,6,1024]{3,2,1,0:T(8,128)(2,1)}, s32[]{:T(128)}, /*index=5*/s32[]{:T(128)}) while((s32[]{:T(128)}, f32[64,864]{1,0:T(8,128)}, bf16[8,64,4096]{2,1,0:T(8,128)(2,1)}, bf16[8,32,6,1024]{3,2,1,0:T(8,128)(2,1)}, s32[]{:T(128)}, ...), condition=%wide.region_13.14_spmd.clone, body=%wide.region_12.13_spmd.clone.sunk | while | flops 467283968 | bytes 40546452 | solution.py:184
  718.9 74.8 %all-reduce.46.cloned.1.call-done = (f32[64,864]{1,0:T(8,128)}, f32[128,1728]{0,1:T(8,128)}) async-done(((f32[64,864]{1,0:T(8,128)}, f32[128,1728]{0,1:T(8,128)}), (f32[64,864]{1,0:T(8,128)}, f32[128,1728]{0,1:T(8,128)})) %all-reduce.46.cloned.1.call-update) | async-done | bytes 1105936 | tf_op jit(solution)/shard_map/psum | solution.py:189
  793.8 28.7 %broadcast_multiply_fusion = f32[65536,128]{1,0:T(8,128)} fusion(f32[128]{0:T(128)S(1)} %copy-done.27, f32[65536]{0:T(1024)S(1)} %convert.13), kind=kLoop, calls=%fused_computation.102 | loop fusion | flops 8388608 | bytes 33817088 | tf_op jit(solution)/shard_map/dot_general | solution.py:127
  822.6 34.6 %all-reduce.37 = (f32[2,64]{1,0:T(2,128)}, f32[128,4]{0,1:T(4,128)}) all-reduce(f32[2,64]{1,0:T(2,128)S(1)} %get-tuple-element.199, f32[128,4]{0,1:T(4,128)S(1)} %get-tuple-element.200), channel_id=1, replica_groups=mesh['dp'=16,'space'=8] {'dp'}, use_global_device_ids=true, to_apply=%region_17.18 | all-reduce | flops 640 | bytes 5120 | tf_op jit(solution)/shard_map/psum | solution.py:188
  857.2 147.9 %all-reduce.44.cloned.1.call-done = (f32[64,864]{1,0:T(8,128)}, f32[128,1728]{0,1:T(8,128)}) async-done(((f32[64,864]{1,0:T(8,128)}, f32[128,1728]{0,1:T(8,128)}), (f32[64,864]{1,0:T(8,128)}, f32[128,1728]{0,1:T(8,128)})) %all-reduce.44.cloned.1.call-update) | async-done | bytes 1105936 | tf_op jit(solution)/shard_map/psum | solution.py:188
  1005.1 558.2 %reduce-scatter.2.cloned.1.call-done = f32[512,128]{1,0:T(8,128)} async-done(((f32[65536,128]{1,0:T(8,128)}), f32[512,128]{1,0:T(8,128)}) %reduce-scatter.2.cloned.1.call-update) | async-done | bytes 262160 | tf_op jit(solution)/shard_map/reduce_scatter | solution.py:126
  (758 shorter events, 425.3 us)
Async XLA Ops:
  8.0 278.8 %copy-start = (bf16[128,1728]{0,1:T(8,128)(2,1)S(1)}, bf16[128,1728]{0,1:T(8,128)(2,1)}, u32[]{:S(2)}) copy-start(bf16[128,1728]{0,1:T(8,128)(2,1)} %param.16) | copy-start | bytes 1327108
  8.0 33.6 %copy-start.4 = (bf16[8,32,4,1024]{3,2,1,0:T(4,128)(2,1)S(1)}, bf16[8,32,4,1024]{3,2,1,0:T(4,128)(2,1)}, u32[]{:S(2)}) copy-start(bf16[8,32,4,1024]{3,2,1,0:T(4,128)(2,1)} %param.12) | copy-start | bytes 6291460
  12.3 15.9 %collective-permute-start.1 = (bf16[8,32,1,1024]{3,1,2,0:T(8,128)(2,1)S(1)}, bf16[8,32,1,1024]{3,1,2,0:T(8,128)(2,1)}, u32[]{:S(2)}, u32[]{:S(2)}) collective-permute-start(bf16[8,32,1,1024]{3,1,2,0:T(8,128)(2,1)S(1)} %copy.53), channel_id=1, source_target_pairs={{1,0},{2,1},{3,2},{4,3},{5,4},{6,5},{7,6},{9,8},{10,9},{11,10},{12... | collective-permute-start | bytes 1572872 | tf_op jit(solution)/shard_map/ppermute | solution.py:21
  14.6 25.1 %collective-permute-start = (bf16[8,32,1,1024]{3,1,2,0:T(8,128)(2,1)}, bf16[8,32,1,1024]{3,1,2,0:T(8,128)(2,1)}, u32[]{:S(2)}, u32[]{:S(2)}) collective-permute-start(bf16[8,32,1,1024]{3,1,2,0:T(8,128)(2,1)} %copy.52), channel_id=1, source_target_pairs={{0,1},{1,2},{2,3},{3,4},{4,5},{5,6},{6,7},{8,9},{9,10},{10,11},{11... | collective-permute-start | bytes 1572872 | tf_op jit(solution)/shard_map/ppermute | solution.py:19
  213.1 24.5 %copy-start.25 = (f32[64]{0:T(128)S(1)}, f32[64]{0:T(128)}, u32[]{:S(2)}) copy-start(f32[64]{0:T(128)} %param.14) | copy-start | bytes 772
  213.1 24.5 %copy-start.26 = (f32[64]{0:T(128)S(1)}, f32[64]{0:T(128)}, u32[]{:S(2)}) copy-start(f32[64]{0:T(128)} %param.15) | copy-start | bytes 772
  262.3 11.6 all-to-all-start
  286.8 5.7 copy-start.3
  296.8 9.3 copy-start.2
  299.1 7.0 copy-start.28
  299.1 7.1 copy-start.29
  306.3 212.4 %copy-start.30 = (f32[1,4]{1,0:T(1,128)}, f32[1,4]{1,0:T(1,128)S(1)}, u32[]{:S(2)}) copy-start(f32[1,4]{1,0:T(1,128)S(1)} %fusion.150) | copy-start | bytes 52
  385.2 9.7 copy-start.24
  428.9 7.2 copy-start.13
  430.2 6.2 copy-start.12
  430.5 7.2 copy-start.11
  431.9 7.2 copy-start.10
  433.2 7.2 copy-start.9
  505.1 13.6 all-to-all-start.1
  508.6 285.1 %all-reduce.46.cloned.1.call-start = ((), (), s32[]{:S(2)}) async-start(), calls=%async_computation.5 | async-start | bytes 2228224 | tf_op jit(solution)/shard_map/psum | solution.py:189
  578.7 215.1 %copy-start.27 = (f32[128]{0:T(128)S(1)}, f32[128]{0:T(128)}, u32[]{:S(2)}) copy-start(f32[128]{0:T(128)} %get-tuple-element.273) | copy-start | bytes 1540
  715.3 289.8 %all-reduce.44.cloned.1.call-start = ((), (), s32[]{:S(2)}) async-start(), calls=%async_computation.4 | async-start | bytes 2228224 | tf_op jit(solution)/shard_map/psum | solution.py:188
  793.7 769.6 %reduce-scatter.2.cloned.1.call-start = ((), (), s32[]{:S(2)}) async-start(), calls=%async_computation.3 | async-start | bytes 33816576 | tf_op jit(solution)/shard_map/reduce_scatter | solution.py:126
  822.6 744.6 %copy-start.1 = (bf16[128,1728]{0,1:T(8,128)(2,1)S(1)}, bf16[128,1728]{0,1:T(8,128)(2,1)}, u32[]{:S(2)}) copy-start(bf16[128,1728]{0,1:T(8,128)(2,1)} %param.16) | copy-start | bytes 1327108
  (28 other events, 82.3 us)
Sparse Core Ops, SparseCore 0:
  715.4 78.2 all-reduce.45
  796.5 208.6 all-reduce.43
Sparse Core Ops, SparseCore 1:
  822.6 740.7 reduce-scatter.1
